TPU v7x, 32 devices: a whole 2x2x4 slice. The times are simulated.
32 devices in a mesh: hist: 16 (over z, y, x), dom: 2 (over core).
Axes of the slice: x: 2, y: 2, z: 4, core: 2. Of those that a mesh axis runs over, the one named last changes fastest.
Arguments:
- coords: float32 [6, 65536], P(None, ('dom', 'hist')), may hold values from -3 to 3
- charge: float32 [65536], P(('dom', 'hist')), may hold values from 0.02 to 0.2
- row_index: int32 [65536], P(('dom', 'hist')), may hold values from 0 to 511, as said below
- block_col: int32 [512], P(('dom', 'hist')), may hold values from 0 to 496
- col_offset: int32 [65536], P(('dom', 'hist')), may hold values from 0 to 15
- transfer_map: float32 [6, 84], replicated
- history: bfloat16 [128, 2, 512, 512], P('hist', None, 'dom'), may hold values from -6 to 6
- retard_index: int32 [128], P('hist'), may hold values from 0 to 16
- retard_frac: float32 [128], P('hist'), may hold values from 0 to 1
- retard_weight: float32 [128], P('hist'), may hold values from 0.005 to 0.05
- z_kernel: float32 [512, 512], P(None, 'dom')
- x_kernel: float32 [512, 512], replicated
Outputs:
- kicked: float32 [6, 65536], P(None, ('dom', 'hist'))
- field: float32 [2, 512, 512], P(None, 'dom', 'hist')
- deposit: float32 [2, 512, 512], P(None, 'dom', 'hist')
Inputs may be any that keep to these rules, and one draw needn't show every extreme that they name: `row_index`: particle i lies in grid slab i // (65536 // 2): its row is that slab's number times 256 plus 0 to 255.
All inputs are finite; a program needn't handle non-finite values.
Results may differ from a plain program's by a relative error of at most 0.0019.
Values may be sent and summed in bfloat16 or wider, within the bound.
No kernel may reach another device: no remote copies, remote signals or barrier semaphores. Data moves between devices by JAX's collectives and lax.ppermute only.
A program may use at most 64 MiB of HBM per device.

v0:
```python
import functools

import jax
import jax.numpy as jnp
from jax import lax
from jax.experimental import pallas as pl
from jax.experimental.pallas import tpu as pltpu
from jax.sharding import PartitionSpec as P

LANES = 128
GROUP = 16
SPAN = 16
SEATS = 8
FIELDS = 4
MORE = 64.0
NT_DIMS = (((1,), (1,)), ((), ()))
VMEM = pl.BlockSpec(memory_space=pltpu.VMEM)
SMEM = pl.BlockSpec(memory_space=pltpu.SMEM)
HBM = pl.BlockSpec(memory_space=pltpu.HBM)
LIMIT = 59 * 1024 * 1024
SMALL = 16 * 1024 * 1024


def call(kernel, out_shape, in_specs, out_specs, scratch=(), flops=0, moved=0, limit=SMALL):
    return pl.pallas_call(
        kernel,
        out_shape=out_shape,
        in_specs=in_specs,
        out_specs=out_specs,
        scratch_shapes=scratch,
        compiler_params=pltpu.CompilerParams(vmem_limit_bytes=limit),
        cost_estimate=pl.CostEstimate(flops=flops, bytes_accessed=moved, transcendentals=0),
    )


def split(value):
    high = value.astype(jnp.bfloat16)
    return high, (value - high.astype(jnp.float32)).astype(jnp.bfloat16)


def seats_of(strips, slabs, blocks):
    if strips == 16 and slabs == 2 and blocks == 2 * SEATS:
        return SEATS, True
    return blocks, False


def strips_met(strip):
    return (SPAN + strip - 2) // strip + 1


def lag_band(lag, near, far):
    row = lax.broadcasted_iota(jnp.int32, (2 * LANES, LANES), 0)
    column = lax.broadcasted_iota(jnp.int32, (2 * LANES, LANES), 1)
    behind = column + LANES - row
    weight = jnp.where(behind == lag, near, jnp.where(behind == lag + 1, far, 0.0))
    return jnp.concatenate(split(weight), axis=1)


def push(coords, transfer, wanted):
    blocks = coords.shape[1] // LANES
    u = [
        jnp.concatenate(
            [coords[i : i + 1, LANES * b : LANES * (b + 1)] for b in range(blocks)], axis=0
        )
        for i in range(6)
    ]
    total = [jnp.full((blocks, LANES), transfer[i, 0], jnp.float32) for i in wanted]
    pairs = {}
    terms = list(u)
    for first in range(6):
        for second in range(first, 6):
            pairs[first, second] = u[first] * u[second]
            terms.append(pairs[first, second])
    for first in range(6):
        for second in range(first, 6):
            for third in range(second, 6):
                terms.append(pairs[first, second] * u[third])
    for column, term in enumerate(terms):
        total = [value + transfer[i, 1 + column] * term for i, value in zip(wanted, total)]
    return total


def push_kernel(transfer, coords, after, pushed):
    del after
    for i, value in enumerate(push(coords, transfer, range(6))):
        pushed[i] = value


def particle_fields(coords, charge, rows, offsets, block_col, transfer, slab_rows):
    blocks = charge.shape[0]
    weight0 = charge[...]
    weight1 = weight0 * push(coords, transfer, [1])[0]
    row_of = lax.broadcasted_iota(jnp.int32, (blocks, LANES), 0)
    column = offsets[...]
    for b in range(blocks):
        column = column + jnp.where(row_of == b, block_col[0, b], 0)
    return lax.rem(rows[...], slab_rows), column, weight0, weight1


def seat_blocks(strips, strip, seats, rounds, block_col, fields, counts, pick, stage):
    row, column, weight0, weight1 = fields
    blocks = row.shape[0]
    nobody = rounds * strips * seats
    meets = strips_met(strip)
    stage[...] = jnp.full(stage.shape, -1.0, jnp.float32)
    for place in range(strips):
        counts[0, place] = 0
    left_out = jnp.int32(0)
    pick_row = lax.broadcasted_iota(jnp.int32, (2 * blocks, LANES), 0)
    lane = lax.broadcasted_iota(jnp.int32, (2 * blocks, LANES), 1)
    wanted = [jnp.zeros((2 * blocks, LANES), jnp.int32)] * meets
    for block in range(blocks):
        start = block_col[0, block]
        first = start // strip
        for step in range(meets):
            place = jnp.minimum(first + step, strips - 1)
            met = (first + step) * strip <= start + (SPAN - 1)
            taken = counts[0, place]
            counts[0, place] = taken + jnp.where(met, 1, 0)
            later = taken // seats
            number = (later * strips + place) * seats + lax.rem(taken, seats)
            number = jnp.where(met, number, nobody)
            left_out = jnp.maximum(left_out, jnp.where(met, later, 0))
            wanted[step] = jnp.where(pick_row >> 1 == block, 2 * number, wanted[step])
            own = column[block : block + 1] - place * strip
            own = jnp.where((own >= 0) & (own < strip), own, -1)
            pieces = [row[block : block + 1], own, weight0[block : block + 1], weight1[block : block + 1]]
            stage[pl.ds(number * FIELDS, FIELDS), :] = jnp.concatenate(
                [piece.astype(jnp.float32) for piece in pieces], axis=0
            )
    lines = 2 * strips * seats
    for turn in range(rounds):
        for left in range(0, lines, LANES):
            line = lane + (turn * lines + left)
            hit = wanted[0] + (pick_row & 1) == line
            for step in range(1, meets):
                hit = hit | (wanted[step] + (pick_row & 1) == line)
            pick[turn, :, left : left + LANES] = jnp.where(hit, 1.0, 0.0).astype(pick.dtype)
    return left_out


def source_kernel(
    strips,
    block_col_from,
    lags_from,
    fracs_from,
    weights_from,
    coords_from,
    charge_from,
    rows_from,
    offsets_from,
    transfer_from,
    history,
    x_kernel,
    packed_to,
    later_to,
    pick_to,
    block_col,
    lags,
    fracs,
    weights,
    coords,
    charge,
    rows,
    offsets,
    transfer,
    frames,
    x_here,
    x_parts,
    s_parts,
    spread_all,
    bands,
    first_bands,
    packed,
    later,
    counts,
    pick,
    stage,
    sems,
):
    count_steps, comps, slab_rows, width = history.shape
    blocks = charge.shape[0]
    strip = width // strips
    spread_rows = comps * strip
    record_rows = packed.shape[1] - spread_rows
    across = packed.shape[2] // LANES
    seats = record_rows * across // FIELDS
    rounds = stage.shape[0] // (FIELDS * strips * seats)
    pairs = [
        (lags_from, lags),
        (fracs_from, fracs),
        (weights_from, weights),
        (block_col_from, block_col),
        (coords_from, coords),
        (charge_from, charge),
        (rows_from, rows),
        (offsets_from, offsets),
        (transfer_from, transfer),
    ]
    for comp in range(comps):
        pairs += [(history.at[t, comp], frames.at[t, comp]) for t in range(count_steps)]
        if comp == 0:
            pairs += [(x_kernel, x_here)]
    fetch = [
        pltpu.make_async_copy(source, target, sems.at[index])
        for index, (source, target) in enumerate(pairs)
    ]
    for copy in fetch:
        copy.start()
    stored = []

    def store(source, target):
        copy = pltpu.make_async_copy(source, target, sems.at[len(fetch) + len(stored)])
        copy.start()
        stored.append(copy)

    for copy in fetch[:3]:
        copy.wait()
    for t in range(count_steps):
        far = weights[0, t] * fracs[0, t]
        near = weights[0, t] * (1.0 - fracs[0, t])
        bands[2 * LANES * t : 2 * LANES * (t + 1)] = lag_band(lags[0, t], near, far)
        first_bands[LANES * t : LANES * (t + 1)] = bands[
            2 * LANES * t + LANES : 2 * LANES * (t + 1)
        ]

    for copy in fetch[3:9]:
        copy.wait()
    row, column, weight0, weight1 = particle_fields(
        coords, charge, rows, offsets, block_col, transfer, slab_rows
    )
    left_out = seat_blocks(
        strips,
        strip,
        seats,
        rounds,
        block_col,
        (row, column, weight0, weight1),
        counts,
        pick,
        stage,
    )
    store(pick, pick_to)
    is_column = lax.rem(lax.broadcasted_iota(jnp.int32, (record_rows, LANES), 0), FIELDS) == 1
    mark = jnp.where(is_column, MORE * left_out.astype(jnp.float32), 0.0)
    for turn in range(rounds):
        for partner in range(strips):
            for side in range(across):
                start = ((turn * strips + partner) * across + side) * record_rows
                value = stage[start : start + record_rows]
                lanes = slice(side * LANES, (side + 1) * LANES)
                if turn == 0:
                    packed[partner, spread_rows:, lanes] = (value + mark).astype(packed.dtype)
                else:
                    later[partner, :, lanes] = value.astype(later.dtype)
    if rounds == 2:
        store(later, later_to)
    store(packed.at[:, spread_rows:], packed_to.at[:, spread_rows:])

    for comp in range(comps):
        first = 9 + comp * (count_steps + 1)
        for copy in fetch[first : first + count_steps]:
            copy.wait()
        here = slice(comp * slab_rows, (comp + 1) * slab_rows)
        part_rows = min(128, slab_rows)
        for top in range(0, slab_rows, part_rows):
            for q in range(width // LANES):
                before = slice(LANES * max(q - 1, 0), LANES * (q + 1))
                steps = [
                    frames[t, comp, top : top + part_rows, before] for t in range(count_steps)
                ]
                both = jnp.dot(
                    jnp.concatenate(steps, axis=1),
                    bands[...] if q else first_bands[...],
                    preferred_element_type=jnp.float32,
                )
                high, low = split(both[:, :LANES] + both[:, LANES:])
                part = slice(comp * slab_rows + top, comp * slab_rows + top + part_rows)
                s_parts[part, LANES * q : LANES * (q + 1)] = high
                s_parts[part, width + LANES * q : width + LANES * (q + 1)] = low
                s_parts[part, 2 * width + LANES * q : 2 * width + LANES * (q + 1)] = high
        if comp == 0:
            fetch[9 + count_steps].wait()
            high, low = split(x_here[...])
            x_parts[:width] = high
            x_parts[width : 2 * width] = high
            x_parts[2 * width :] = low
        spread = jnp.dot(s_parts[here], x_parts[...], preferred_element_type=jnp.float32)
        if strip % 16 == 0:
            turned = spread.astype(packed.dtype).T
            part = slice(comp * strip, (comp + 1) * strip)
            for partner in range(strips):
                packed[partner, part, :slab_rows] = turned[
                    partner * strip : (partner + 1) * strip
                ]
            store(packed.at[:, part], packed_to.at[:, part])
        else:
            spread_all[comp] = spread.T
    if strip % 16:
        for partner in range(strips):
            part = slice(partner * strip, (partner + 1) * strip)
            both = jnp.concatenate([spread_all[comp, part] for comp in range(comps)], axis=0)
            packed[partner, :spread_rows, :slab_rows] = both.astype(packed.dtype)
        store(packed.at[:, :spread_rows], packed_to.at[:, :spread_rows])
    for copy in stored:
        copy.wait()


def join_kernel(slabs, spread_rows, z_kernel, arrived, kept, *sent):
    slab_rows = z_kernel.shape[0] // slabs
    extra_rows = kept.shape[0] - spread_rows if sent else 0
    total = arrived[0, :spread_rows, :slab_rows].astype(jnp.float32)
    for sender in range(1, arrived.shape[0]):
        total = total + arrived[sender, :spread_rows, :slab_rows].astype(jnp.float32)
    high, low = split(total)
    left = jnp.concatenate([high, low, high], axis=1)

    def part(slab):
        start = pl.multiple_of(slab * slab_rows, slab_rows)
        z_high, z_low = split(z_kernel[pl.ds(start, slab_rows), :])
        right = jnp.concatenate([z_high, z_high, z_low], axis=1)
        return lax.dot_general(left, right, NT_DIMS, preferred_element_type=jnp.float32)

    if sent:
        me = lax.axis_index("dom")
        sent[0][:spread_rows] = part(1 - me)
        kept[:spread_rows] = part(me)
        if extra_rows:
            records = jnp.max(arrived[:, spread_rows:].astype(jnp.float32), axis=0)
            is_column = lax.rem(lax.broadcasted_iota(jnp.int32, records.shape, 0), FIELDS) == 1
            most = jnp.max(jnp.where(is_column, records, -1.0))
            flag = jnp.full((extra_rows, slab_rows), jnp.where(most >= MORE - 1.0, 1.0, 0.0))
            sent[0][spread_rows:] = flag
            kept[spread_rows:] = flag
    else:
        for slab in range(slabs):
            kept[slab] = part(slab)


def unpack_kernel(spread_rows, arrived, records, chosen):
    senders = arrived.shape[0]
    record_rows = arrived.shape[1] - spread_rows
    across = arrived.shape[2] // LANES
    blocks = record_rows * across // FIELDS
    line = lax.broadcasted_iota(jnp.int32, (record_rows, LANES), 0)
    is_column = lax.rem(line, FIELDS) == 1
    first_line = lax.broadcasted_iota(jnp.int32, (record_rows, 1), 0)
    first_column = lax.rem(first_line, FIELDS) == 1
    masks = []
    for sender in range(senders):
        mask = jnp.float32(0.0)
        for side in range(across):
            lanes = slice(side * LANES, (side + 1) * LANES)
            value = arrived[sender, spread_rows:, lanes].astype(jnp.float32)
            value = jnp.where(is_column & (value >= MORE - 1.0), value - MORE, value)
            records[sender, side * record_rows : (side + 1) * record_rows] = value
            taken = first_column & (jnp.max(value, axis=1, keepdims=True) >= 0.0)
            seat = first_line // FIELDS + side * (record_rows // FIELDS)
            bit = jnp.left_shift(jnp.ones_like(seat), seat).astype(jnp.float32)
            mask = mask + jnp.sum(jnp.where(taken, bit, 0.0))
        masks.append(mask.astype(jnp.int32))
    records[senders] = jnp.full(records.shape[1:], -1.0, jnp.float32)
    count = jnp.int32(0)
    for sender in range(senders):
        for block in range(blocks):
            chosen[1 + count] = sender * blocks + block
            count = count + ((masks[sender] >> block) & 1)
    chosen[0] = (count + (GROUP - 1)) // GROUP
    for member in range(GROUP):
        chosen[1 + count + member] = senders * blocks


def read_group(blocks, chosen, records, group):
    where = []
    for member in range(GROUP):
        block = chosen[1 + group * GROUP + member]
        where.append((block // blocks, lax.rem(block, blocks)))

    lines = jnp.concatenate(
        [records[sender, pl.ds(own * FIELDS, FIELDS), :] for sender, own in where], axis=1
    )

    def field(index):
        return lines[index : index + 1]

    return where, field


def one_hot(index, size):
    iota = lax.broadcasted_iota(jnp.int32, (size, index.shape[1]), 0).astype(jnp.float32)
    return iota == index


def one_hot_rows(row, size):
    iota = lax.broadcasted_iota(jnp.int32, (size, row.shape[1]), 0)
    if size <= 256:
        hit = iota.astype(jnp.bfloat16) == row.astype(jnp.bfloat16)
        return jnp.where(hit, jnp.bfloat16(1.0), jnp.bfloat16(0.0))
    return jnp.where(iota.astype(jnp.float32) == row, 1.0, 0.0).astype(jnp.bfloat16)


def deposit_kernel(blocks, chosen, records, after, *refs):
    del after
    extra, (deposit, total) = refs[:-2], refs[-2:]
    strip, slab_rows = deposit.shape[1:]
    total[...] = jnp.zeros_like(total)

    def one_group(group, carry):
        _, field = read_group(blocks, chosen, records, group)
        hit = one_hot(field(1), strip)
        weighted = [jnp.where(hit, field(2 + comp), 0.0) for comp in range(2)]
        total[...] += lax.dot_general(
            one_hot_rows(field(0), slab_rows),
            jnp.concatenate(weighted, axis=0).astype(jnp.bfloat16),
            NT_DIMS,
            preferred_element_type=jnp.float32,
        )
        return carry

    lax.fori_loop(0, chosen[0], one_group, 0)
    turned = total[...].T
    for comp in range(2):
        own = turned[comp * strip : (comp + 1) * strip]
        deposit[comp] = own + extra[0][comp] if extra else own


def sample_kernel(blocks, chosen, records, *refs):
    parts, (field_out, samples, flag, found_all) = refs[:-4], refs[-4:]
    strip, slab_rows = field_out.shape[1:]
    if len(parts) == 1:
        total = parts[0][0]
        for slab in range(1, parts[0].shape[0]):
            total = total + parts[0][slab]
    else:
        total = parts[0][: 2 * strip] + parts[1][: 2 * strip]
    if len(parts) == 2 and parts[0].shape[0] > 2 * strip:
        most = jnp.max(jnp.maximum(parts[0][2 * strip :], parts[1][2 * strip :]))
        flag[0] = jnp.where(most > 0.5, 1, 0)
    else:
        flag[0] = 0
    field_out[0] = total[:strip]
    field_out[1] = total[strip:]
    rounded = total.astype(jnp.bfloat16)
    found_all[...] = jnp.zeros_like(found_all)

    def one_group(group, carry):
        where, field = read_group(blocks, chosen, records, group)
        row_hot = one_hot_rows(field(0), slab_rows)
        found = jnp.dot(rounded, row_hot, preferred_element_type=jnp.float32)
        hit = one_hot(field(1), strip)
        values = []
        for comp in range(2):
            picked = jnp.where(hit, found[comp * strip : (comp + 1) * strip], 0.0)
            values.append(jnp.sum(picked, axis=0, keepdims=True))
        values = jnp.concatenate(values, axis=0)
        for member, (sender, own) in enumerate(where):
            found_all[sender, pl.ds(2 * own, 2), :] = values[
                :, LANES * member : LANES * (member + 1)
            ]
        return carry

    lax.fori_loop(0, chosen[0], one_group, 0)
    samples[...] = found_all[: samples.shape[0]].astype(samples.dtype)


def found_for_blocks(pick, received):
    flat = received[...].reshape(received.shape[0] * received.shape[1], LANES)
    return jnp.dot(pick, flat, preferred_element_type=jnp.float32)


def more_kernel(pick, received, more):
    more[...] = found_for_blocks(pick[1], received)


def kick_kernel(pick, pushed, received, *refs):
    more, kicked = refs[:-1], refs[-1]
    blocks = pushed.shape[1]
    values = [pushed[i] for i in range(6)]
    total = found_for_blocks(pick[0], received)
    if more:
        total = total + more[0][...]
    for block in range(blocks):
        lines = [value[block : block + 1] for value in values]
        lines[5] = lines[5] + 0.5 * total[2 * block : 2 * block + 1]
        lines[1] = lines[1] + 0.5 * total[2 * block + 1 : 2 * block + 2]
        kicked[:, LANES * block : LANES * (block + 1)] = jnp.concatenate(lines, axis=0)


def local(
    coords,
    charge,
    row_index,
    block_col,
    col_offset,
    transfer_map,
    history,
    retard_index,
    retard_frac,
    retard_weight,
    z_kernel,
    x_kernel,
):
    strips = lax.axis_size("hist")
    slabs = lax.axis_size("dom")
    count_steps, comps, slab_rows, width = history.shape
    strip = width // strips
    particles = coords.shape[1]
    blocks = block_col.shape[0]
    tile = (blocks, LANES)
    spread_rows = comps * strip
    row_lanes = max(slab_rows, LANES)
    seats, second_round = seats_of(strips, slabs, blocks)
    rounds = 2 if second_round else 1
    record_rows = FIELDS * seats * LANES // row_lanes
    packed_rows = spread_rows + record_rows

    f32, bf16 = jnp.float32, jnp.bfloat16
    packed, later, pick = call(
        functools.partial(source_kernel, strips),
        (
            jax.ShapeDtypeStruct((strips, packed_rows, row_lanes), bf16),
            jax.ShapeDtypeStruct((strips, record_rows, row_lanes), bf16),
            jax.ShapeDtypeStruct((rounds, comps * blocks, comps * strips * seats), bf16),
        ),
        [HBM] * 11,
        (HBM, HBM, HBM),
        [
            pltpu.SMEM((1, blocks), jnp.int32),
            pltpu.SMEM((1, count_steps), jnp.int32),
            pltpu.SMEM((1, count_steps), f32),
            pltpu.SMEM((1, count_steps), f32),
            pltpu.VMEM(coords.shape, f32),
            pltpu.VMEM(tile, f32),
            pltpu.VMEM(tile, jnp.int32),
            pltpu.VMEM(tile, jnp.int32),
            pltpu.SMEM(transfer_map.shape, f32),
            pltpu.VMEM(history.shape, bf16),
            pltpu.VMEM((width, width), f32),
            pltpu.VMEM((3 * width, width), bf16),
            pltpu.VMEM((comps * slab_rows, 3 * width), bf16),
            pltpu.VMEM((comps, width, slab_rows), f32),
            pltpu.VMEM((2 * LANES * count_steps, 2 * LANES), bf16),
            pltpu.VMEM((LANES * count_steps, 2 * LANES), bf16),
            pltpu.VMEM((strips, packed_rows, row_lanes), bf16),
            pltpu.VMEM((strips, record_rows, row_lanes), bf16),
            pltpu.SMEM((1, strips), jnp.int32),
            pltpu.VMEM((rounds, comps * blocks, comps * strips * seats), bf16),
            pltpu.VMEM((FIELDS * (rounds * strips * seats + 2), LANES), f32),
            pltpu.SemaphoreType.DMA((16 + comps * count_steps,)),
        ],
        flops=6 * comps * slab_rows * width * width,
        moved=history.size * 2 + x_kernel.size * 4,
        limit=LIMIT,
    )(
        block_col.reshape(1, blocks),
        retard_index.reshape(1, count_steps),
        retard_frac.reshape(1, count_steps),
        retard_weight.reshape(1, count_steps),
        coords,
        charge.reshape(tile),
        row_index.reshape(tile),
        col_offset.reshape(tile),
        transfer_map,
        history,
        x_kernel,
    )
    arrived = lax.all_to_all(packed, "hist", 0, 0, tiled=True)

    part = jax.ShapeDtypeStruct((spread_rows + (8 if second_round else 0), slab_rows), f32)
    parts = call(
        functools.partial(join_kernel, slabs, spread_rows),
        (part, part) if slabs == 2 else jax.ShapeDtypeStruct((slabs,) + part.shape, f32),
        [VMEM, VMEM],
        (VMEM, VMEM) if slabs == 2 else VMEM,
        flops=1 << 27,
        moved=1 << 20,
    )(z_kernel, arrived)
    if slabs == 2:
        kept, sent = parts
        parts = [kept, lax.ppermute(sent, "dom", [(0, 1), (1, 0)])]
    else:
        parts = [lax.all_to_all(parts, "dom", 0, 0, tiled=True)]

    def unpack(arrived, spread_rows):
        return call(
            functools.partial(unpack_kernel, spread_rows),
            (
                jax.ShapeDtypeStruct((strips + 1, FIELDS * seats, LANES), f32),
                jax.ShapeDtypeStruct((strips * seats + 32,), jnp.int32),
            ),
            [VMEM],
            (VMEM, SMEM),
            flops=1 << 20,
            moved=1 << 20,
        )(arrived)

    def sample(chosen, records, parts):
        return call(
            functools.partial(sample_kernel, seats),
            (
                jax.ShapeDtypeStruct((comps, strip, slab_rows), f32),
                jax.ShapeDtypeStruct((strips, comps * seats, LANES), bf16),
                jax.ShapeDtypeStruct((8,), jnp.int32),
            ),
            [SMEM, VMEM] + [VMEM] * len(parts),
            (VMEM, VMEM, SMEM),
            [pltpu.VMEM((strips + 1, comps * seats, LANES), f32)],
            flops=1 << 29,
            moved=1 << 20,
        )(chosen, records, *parts)

    def deposits(chosen, records, after, *extra):
        return call(
            functools.partial(deposit_kernel, seats),
            jax.ShapeDtypeStruct((comps, strip, slab_rows), f32),
            [SMEM, VMEM, HBM] + [VMEM] * len(extra),
            VMEM,
            [pltpu.VMEM((slab_rows, comps * strip), f32)],
            flops=1 << 29,
            moved=1 << 20,
        )(chosen, records, after, *extra)

    def exchange(value):
        return lax.all_to_all(value, "hist", 0, 0, tiled=True)

    records, chosen = unpack(arrived, spread_rows)
    field, samples, flag = sample(chosen, records, parts)
    more, extra = [], []
    if second_round:

        def another(later, field, pick):
            records, chosen = unpack(exchange(later), 0)
            whole = field.reshape(1, spread_rows, slab_rows)
            _, samples, _ = sample(chosen, records, [whole])
            more = call(
                more_kernel,
                jax.ShapeDtypeStruct((comps * blocks, LANES), f32),
                [VMEM, VMEM],
                VMEM,
            )(pick, exchange(samples))
            return more, deposits(chosen, records, samples)

        def nothing(later, field, pick):
            return jnp.zeros((comps * blocks, LANES), f32), jnp.zeros(field.shape, f32)

        found, left = lax.cond(flag[0] > 0, another, nothing, later, field, pick)
        more, extra = [found], [left]
    received = exchange(samples)
    deposit = deposits(chosen, records, samples, *extra)
    pushed = call(
        push_kernel,
        jax.ShapeDtypeStruct((6,) + tile, f32),
        [SMEM, VMEM, HBM],
        VMEM,
        flops=1200 * particles,
        moved=1 << 18,
    )(transfer_map, coords, samples)
    kicked = call(
        kick_kernel,
        jax.ShapeDtypeStruct((6, particles), f32),
        [VMEM] * (3 + len(more)),
        VMEM,
        flops=1 << 16,
        moved=1 << 18,
    )(pick, pushed, received, *more)
    return kicked, jnp.transpose(field, (0, 2, 1)), jnp.transpose(deposit, (0, 2, 1))


def solution(mesh):
    return jax.shard_map(
        local,
        mesh=mesh,
        in_specs=(
            P(None, ("dom", "hist")),
            P(("dom", "hist")),
            P(("dom", "hist")),
            P(("dom", "hist")),
            P(("dom", "hist")),
            P(),
            P("hist", None, "dom", None),
            P("hist"),
            P("hist"),
            P("hist"),
            P(None, "dom"),
            P(),
        ),
        out_specs=(P(None, ("dom", "hist")), P(None, "dom", "hist"), P(None, "dom", "hist")),
        check_vma=False,
    )
```

profile of v0, /device:TPU:0, one launch (start us, length us, event | category | flops | bytes accessed | tf_op | source)
XLA Modules:
  0.0 49.6 jit_solution(3282971823631175595)
XLA Ops:
  0.6 0.0 copy-start
  0.6 6.6 %shard_map.139 = (bf16[16,80,256]{2,1,0:T(8,128)(2,1)}, bf16[16,16,256]{2,1,0:T(8,128)(2,1)S(1)}, bf16[2,32,256]{2,1,0:T(8,128)(2,1)S(1)}) custom-call(s32[1,16]{1,0:T(1,128)} %bitcast.16, s32[1,8]{1,0:T(1,128)} %bitcast.17, f32[1,8]{1,0:T(1,128)} %bitcast.18, f32[1,8]{1,0:T(1,128)} %bitcast.19, f32[6,2048]{1,0:T(8,128)} %coords.1, f32[16,128]{1,0:T(8,128)} %bitcast.13, ...), custom_call_target="tpu_custom_call" | custom-call | flops 805306368 | bytes 5242880 | tf_op jit(solution)/shard_map/pallas_call | solution.py:518
  7.3 27.1 %all_to_all.19.arrived = bf16[16,80,256]{2,1,0:T(8,128)(2,1)S(1)} all-to-all(bf16[16,80,256]{2,1,0:T(8,128)(2,1)} %get-tuple-element.28), channel_id=1, replica_groups=mesh['hist'=16,'dom'=2] {'hist'}, dimensions={0} | all-to-all | bytes 1310720 | tf_op jit(solution)/shard_map/all_to_all | solution.py:567
  34.3 0.0 copy-done
  34.3 0.0 copy-start.1
  34.3 0.0 copy-start.2
  34.3 0.4 shard_map.141
  34.7 0.1 collective-permute-start
  34.8 1.1 %shard_map.140 = (f32[17,32,128]{2,1,0:T(8,128)S(1)}, s32[160]{0:T(256)S(1)}) custom-call(bf16[16,80,256]{2,1,0:T(8,128)(2,1)S(1)} %all_to_all.19.arrived), custom_call_target="tpu_custom_call" | custom-call | flops 1048576 | bytes 1048576 | tf_op jit(solution)/shard_map/pallas_call | solution.py:585
  35.9 0.2 collective-permute-done.refs_1_
  36.1 1.7 %shard_map.142 = (f32[2,32,256]{2,1,0:T(8,128)}, bf16[16,16,128]{2,1,0:T(8,128)(2,1)}, s32[8]{0:T(128)S(1)}) custom-call(s32[160]{0:T(256)S(1)} %get-tuple-element.29.chosen, f32[17,32,128]{2,1,0:T(8,128)S(1)} %get-tuple-element.30.records, f32[72,256]{1,0:T(8,128)S(1)} %get-tuple-element.31.refs_0_, f32[72,256]{1,0:T(8,128)S(1)} %collective-permute-done.refs_1_), custom_call_target="tpu_custom_call" | custom-call | flops 536870912 | bytes 1048576 | tf_op jit(solution)/shard_map/pallas_call | solution.py:598
  37.8 3.5 %all-to-all-start.3 = ((bf16[16,16,128]{2,1,0:T(8,128)(2,1)}), bf16[16,16,128]{2,1,0:T(8,128)(2,1)S(1)}, u32[]{:S(2)}, u32[]{:S(2)}) async-start(bf16[16,16,128]{2,1,0:T(8,128)(2,1)} %get-tuple-element.33.after), calls=%async_computation.3 | async-start | bytes 131072 | tf_op jit(solution)/shard_map/all_to_all | solution.py:624
  41.3 0.0 copy-done.1
  41.4 0.0 copy-done.2
  41.4 1.1 %shard_map.143.pushed = f32[6,16,128]{2,1,0:T(8,128)S(1)} custom-call(f32[6,84]{1,0:T(8,128)S(1)} %copy-done.2, f32[6,2048]{1,0:T(8,128)S(1)} %copy-done.1, bf16[16,16,128]{2,1,0:T(8,128)(2,1)} %get-tuple-element.33.after), custom_call_target="tpu_custom_call" | custom-call | flops 2457600 | bytes 262144 | tf_op jit(solution)/shard_map/pallas_call | solution.py:650
  42.4 1.7 %shard_map.145 = f32[2,32,256]{2,1,0:T(8,128)} custom-call(s32[160]{0:T(256)S(1)} %get-tuple-element.29.chosen, f32[17,32,128]{2,1,0:T(8,128)S(1)} %get-tuple-element.30.records, bf16[16,16,128]{2,1,0:T(8,128)(2,1)} %get-tuple-element.33.after, f32[2,32,256]{2,1,0:T(8,128)S(1)} %get-tuple-element.38.refs_0_), custom_call_target="tpu_custom_call" | custom-call | flops 536870912 | bytes 1048576 | tf_op jit(solution)/shard_map/pallas_call | solution.py:613
  44.2 4.7 %all-to-all-done.3.received = bf16[16,16,128]{2,1,0:T(8,128)(2,1)S(1)} async-done(((bf16[16,16,128]{2,1,0:T(8,128)(2,1)}), bf16[16,16,128]{2,1,0:T(8,128)(2,1)S(1)}, u32[]{:S(2)}, u32[]{:S(2)}) %all-to-all-start.3) | async-done | bytes 65568 | tf_op jit(solution)/shard_map/all_to_all | solution.py:624
  48.9 0.8 %shard_map.144 = f32[6,2048]{1,0:T(8,128)} custom-call(bf16[2,32,256]{2,1,0:T(8,128)(2,1)S(1)} %get-tuple-element.27.pick, f32[6,16,128]{2,1,0:T(8,128)S(1)} %shard_map.143.pushed, bf16[16,16,128]{2,1,0:T(8,128)(2,1)S(1)} %all-to-all-done.3.received, f32[32,128]{1,0:T(8,128)S(1)} %get-tuple-element.37.refs_0_), custom_call_target="tpu_custom_call" | custom-call | flops 65536 | bytes 262144 | tf_op jit(solution)/shard_map/pallas_call | solution.py:658
  (3 shorter events, 0.0 us)
Async XLA Ops:
  0.6 33.7 %copy-start = (f32[512,256]{1,0:T(8,128)S(1)}, f32[512,256]{1,0:T(8,128)}, u32[]{:S(2)}) copy-start(f32[512,256]{1,0:T(8,128)} %z_kernel.1) | copy-start | bytes 1572868
  34.3 7.0 %copy-start.1 = (f32[6,2048]{1,0:T(8,128)S(1)}, f32[6,2048]{1,0:T(8,128)}, u32[]{:S(2)}) copy-start(f32[6,2048]{1,0:T(8,128)} %coords.1) | copy-start | bytes 147460
  34.3 7.0 %copy-start.2 = (f32[6,84]{1,0:T(8,128)S(1)}, f32[6,84]{1,0:T(8,128)}, u32[]{:S(2)}) copy-start(f32[6,84]{1,0:T(8,128)} %transfer.1) | copy-start | bytes 6052
  34.7 1.3 %collective-permute-start = (f32[72,256]{1,0:T(8,128)S(1)}, f32[72,256]{1,0:T(8,128)S(1)}, u32[]{:S(2)}, u32[]{:S(2)}) collective-permute-start(f32[72,256]{1,0:T(8,128)S(1)} %get-tuple-element.32), channel_id=1, source_target_pairs={{0,1},{1,0},{2,3},{3,2},{4,5},{5,4},{6,7},{7,6},{8,9},{9,8},{10,11... | collective-permute-start | bytes 221192 | tf_op jit(solution)/shard_map/ppermute | solution.py:580
  37.8 11.0 %all-to-all-start.3 = ((bf16[16,16,128]{2,1,0:T(8,128)(2,1)}), bf16[16,16,128]{2,1,0:T(8,128)(2,1)S(1)}, u32[]{:S(2)}, u32[]{:S(2)}) async-start(bf16[16,16,128]{2,1,0:T(8,128)(2,1)} %get-tuple-element.33.after), calls=%async_computation.3 | async-start | bytes 131072 | tf_op jit(solution)/shard_map/all_to_all | solution.py:624
where the time goes:
time: 50.1 us; the launch traced here: 49.6 us
  blocking collectives  27.1 us (54%)
  Pallas kernels  13.4 us (27%)
  waiting for transfers between devices  4.84 us (10%)
  starting transfers between devices  3.58 us (7%)
  between operations  0.75 us (1%)
    all_to_all x1, blocking collectives, local(): arrived = lax.all_to_all(packed, 'hist', 0, 0, tiled=True)  27.1 us
    pallas_call x1, Pallas kernels, local(): call(functools.partial(source_kernel, strips), (jax.ShapeDtypeStruct((str...  6.63 us
    all_to_all x1, waiting for transfers between devices, exchange(): return lax.all_to_all(value, 'hist', 0, 0, tiled=True)  4.68 us
    all_to_all x1, starting transfers between devices, exchange(): return lax.all_to_all(value, 'hist', 0, 0, tiled=True)  3.51 us
    pallas_call x1, Pallas kernels, deposits(): call(functools.partial(deposit_kernel, seats), jax.ShapeDtypeStruct((comp...  1.72 us
    pallas_call x1, Pallas kernels, sample(): call(functools.partial(sample_kernel, seats), (jax.ShapeDtypeStruct((comp...  1.68 us
    pallas_call x1, Pallas kernels, unpack(): call(functools.partial(unpack_kernel, spread_rows), (jax.ShapeDtypeStruct...  1.09 us
    pallas_call x1, Pallas kernels, local(): call(push_kernel, jax.ShapeDtypeStruct((6,) + tile, f32), [SMEM, VMEM, HB...  1.08 us
  transfers between devices with their start and end apart: 2, of which 2 were waited for; matrix products, arithmetic and copies ran while one was open for 0% of the time, Pallas kernels for 8%

commit v1 on v0

--- a/solution.py
+++ b/solution.py
@@ -109,7 +109,10 @@
     pick_row = lax.broadcasted_iota(jnp.int32, (2 * blocks, LANES), 0)
     lane = lax.broadcasted_iota(jnp.int32, (2 * blocks, LANES), 1)
     wanted = [jnp.zeros((2 * blocks, LANES), jnp.int32)] * meets
+    is_column = lax.broadcasted_iota(jnp.int32, (FIELDS, LANES), 0) == 1
+    fields = [field.astype(jnp.float32) for field in (row, column, weight0, weight1)]
     for block in range(blocks):
+        tile = jnp.concatenate([field[block : block + 1] for field in fields], axis=0)
         start = block_col[0, block]
         first = start // strip
         for step in range(meets):
@@ -122,12 +125,9 @@
             number = jnp.where(met, number, nobody)
             left_out = jnp.maximum(left_out, jnp.where(met, later, 0))
             wanted[step] = jnp.where(pick_row >> 1 == block, 2 * number, wanted[step])
-            own = column[block : block + 1] - place * strip
-            own = jnp.where((own >= 0) & (own < strip), own, -1)
-            pieces = [row[block : block + 1], own, weight0[block : block + 1], weight1[block : block + 1]]
-            stage[pl.ds(number * FIELDS, FIELDS), :] = jnp.concatenate(
-                [piece.astype(jnp.float32) for piece in pieces], axis=0
-            )
+            own = tile - (place * strip).astype(jnp.float32)
+            own = jnp.where((own >= 0.0) & (own < strip), own, -1.0)
+            stage[pl.ds(number * FIELDS, FIELDS), :] = jnp.where(is_column, own, tile)
     lines = 2 * strips * seats
     for turn in range(rounds):
         for left in range(0, lines, LANES):
@@ -214,7 +214,7 @@
         copy.start()
         stored.append(copy)
 
-    for copy in fetch[:3]:
+    for copy in fetch[:9]:
         copy.wait()
     for t in range(count_steps):
         far = weights[0, t] * fracs[0, t]
@@ -224,8 +224,6 @@
             2 * LANES * t + LANES : 2 * LANES * (t + 1)
         ]
 
-    for copy in fetch[3:9]:
-        copy.wait()
     row, column, weight0, weight1 = particle_fields(
         coords, charge, rows, offsets, block_col, transfer, slab_rows
     )
@@ -240,7 +238,6 @@
         pick,
         stage,
     )
-    store(pick, pick_to)
     is_column = lax.rem(lax.broadcasted_iota(jnp.int32, (record_rows, LANES), 0), FIELDS) == 1
     mark = jnp.where(is_column, MORE * left_out.astype(jnp.float32), 0.0)
     for turn in range(rounds):
@@ -253,9 +250,6 @@
                     packed[partner, spread_rows:, lanes] = (value + mark).astype(packed.dtype)
                 else:
                     later[partner, :, lanes] = value.astype(later.dtype)
-    if rounds == 2:
-        store(later, later_to)
-    store(packed.at[:, spread_rows:], packed_to.at[:, spread_rows:])
 
     for comp in range(comps):
         first = 9 + comp * (count_steps + 1)
@@ -280,6 +274,10 @@
                 s_parts[part, width + LANES * q : width + LANES * (q + 1)] = low
                 s_parts[part, 2 * width + LANES * q : 2 * width + LANES * (q + 1)] = high
         if comp == 0:
+            store(pick, pick_to)
+            if rounds == 2:
+                store(later, later_to)
+            store(packed.at[:, spread_rows:], packed_to.at[:, spread_rows:])
             fetch[9 + count_steps].wait()
             high, low = split(x_here[...])
             x_parts[:width] = high

time: 50.1 us -> 50.3 us (level)
  Pallas kernels: 13.4 us -> 14.2 us
  transfers between devices with their start and end apart: 2 -> 2, of which waited for: 2 -> 2; matrix products, arithmetic and copies ran while one was open for 0% -> 0% of each run, Pallas kernels for 8% -> 9%
where the time goes in v1:
time: 50.3 us; the launch traced here: 50 us
  blocking collectives  27.1 us (54%)
  Pallas kernels  14.2 us (28%)
  waiting for transfers between devices  4.39 us (9%)
  starting transfers between devices  3.58 us (7%)
  between operations  0.75 us (1%)
    all_to_all x1, blocking collectives, local(): arrived = lax.all_to_all(packed, 'hist', 0, 0, tiled=True)  27.1 us
    pallas_call x1, Pallas kernels, local(): call(functools.partial(source_kernel, strips), (jax.ShapeDtypeStruct((str...  6.63 us
    all_to_all x1, waiting for transfers between devices, exchange(): return lax.all_to_all(value, 'hist', 0, 0, tiled=True)  4.24 us
    all_to_all x1, starting transfers between devices, exchange(): return lax.all_to_all(value, 'hist', 0, 0, tiled=True)  3.51 us
    pallas_call x1, Pallas kernels, deposits(): call(functools.partial(deposit_kernel, seats), jax.ShapeDtypeStruct((comp...  2.17 us
    pallas_call x1, Pallas kernels, sample(): call(functools.partial(sample_kernel, seats), (jax.ShapeDtypeStruct((comp...  2.03 us
    pallas_call x1, Pallas kernels, unpack(): call(functools.partial(unpack_kernel, spread_rows), (jax.ShapeDtypeStruct...  1.09 us
    pallas_call x1, Pallas kernels, local(): call(push_kernel, jax.ShapeDtypeStruct((6,) + tile, f32), [SMEM, VMEM, HB...  1.08 us
  transfers between devices with their start and end apart: 2, of which 2 were waited for; matrix products, arithmetic and copies ran while one was open for 0% of the time, Pallas kernels for 9%

profile of v1, /device:TPU:0, one launch (start us, length us, event | category | flops | bytes accessed | tf_op | source)
XLA Modules:
  0.0 50.0 jit_solution(10059603729893264554)
XLA Ops:
  0.6 0.0 copy-start
  0.6 6.6 %shard_map.139 = (bf16[16,80,256]{2,1,0:T(8,128)(2,1)}, bf16[16,16,256]{2,1,0:T(8,128)(2,1)S(1)}, bf16[2,32,256]{2,1,0:T(8,128)(2,1)S(1)}) custom-call(s32[1,16]{1,0:T(1,128)} %bitcast.16, s32[1,8]{1,0:T(1,128)} %bitcast.17, f32[1,8]{1,0:T(1,128)} %bitcast.18, f32[1,8]{1,0:T(1,128)} %bitcast.19, f32[6,2048]{1,0:T(8,128)} %coords.1, f32[16,128]{1,0:T(8,128)} %bitcast.13, ...), custom_call_target="tpu_custom_call" | custom-call | flops 805306368 | bytes 5242880 | tf_op jit(solution)/shard_map/pallas_call | solution.py:516
  7.3 27.1 %all_to_all.19.arrived = bf16[16,80,256]{2,1,0:T(8,128)(2,1)S(1)} all-to-all(bf16[16,80,256]{2,1,0:T(8,128)(2,1)} %get-tuple-element.28), channel_id=1, replica_groups=mesh['hist'=16,'dom'=2] {'hist'}, dimensions={0} | all-to-all | bytes 1310720 | tf_op jit(solution)/shard_map/all_to_all | solution.py:565
  34.3 0.0 copy-done
  34.3 0.0 copy-start.1
  34.3 0.0 copy-start.2
  34.3 0.4 shard_map.141
  34.7 0.1 collective-permute-start
  34.8 1.1 %shard_map.140 = (f32[17,32,128]{2,1,0:T(8,128)S(1)}, s32[160]{0:T(256)S(1)}) custom-call(bf16[16,80,256]{2,1,0:T(8,128)(2,1)S(1)} %all_to_all.19.arrived), custom_call_target="tpu_custom_call" | custom-call | flops 1048576 | bytes 1048576 | tf_op jit(solution)/shard_map/pallas_call | solution.py:583
  35.9 0.2 collective-permute-done.refs_1_
  36.1 2.0 %shard_map.142 = (f32[2,32,256]{2,1,0:T(8,128)}, bf16[16,16,128]{2,1,0:T(8,128)(2,1)}, s32[8]{0:T(128)S(1)}) custom-call(s32[160]{0:T(256)S(1)} %get-tuple-element.29.chosen, f32[17,32,128]{2,1,0:T(8,128)S(1)} %get-tuple-element.30.records, f32[72,256]{1,0:T(8,128)S(1)} %get-tuple-element.31.refs_0_, f32[72,256]{1,0:T(8,128)S(1)} %collective-permute-done.refs_1_), custom_call_target="tpu_custom_call" | custom-call | flops 536870912 | bytes 1048576 | tf_op jit(solution)/shard_map/pallas_call | solution.py:596
  38.2 3.5 %all-to-all-start.3 = ((bf16[16,16,128]{2,1,0:T(8,128)(2,1)}), bf16[16,16,128]{2,1,0:T(8,128)(2,1)S(1)}, u32[]{:S(2)}, u32[]{:S(2)}) async-start(bf16[16,16,128]{2,1,0:T(8,128)(2,1)} %get-tuple-element.33.after), calls=%async_computation.3 | async-start | bytes 131072 | tf_op jit(solution)/shard_map/all_to_all | solution.py:622
  41.7 0.0 copy-done.1
  41.7 0.0 copy-done.2
  41.7 1.1 %shard_map.143.pushed = f32[6,16,128]{2,1,0:T(8,128)S(1)} custom-call(f32[6,84]{1,0:T(8,128)S(1)} %copy-done.2, f32[6,2048]{1,0:T(8,128)S(1)} %copy-done.1, bf16[16,16,128]{2,1,0:T(8,128)(2,1)} %get-tuple-element.33.after), custom_call_target="tpu_custom_call" | custom-call | flops 2457600 | bytes 262144 | tf_op jit(solution)/shard_map/pallas_call | solution.py:648
  42.8 2.2 %shard_map.145 = f32[2,32,256]{2,1,0:T(8,128)} custom-call(s32[160]{0:T(256)S(1)} %get-tuple-element.29.chosen, f32[17,32,128]{2,1,0:T(8,128)S(1)} %get-tuple-element.30.records, bf16[16,16,128]{2,1,0:T(8,128)(2,1)} %get-tuple-element.33.after, f32[2,32,256]{2,1,0:T(8,128)S(1)} %get-tuple-element.38.refs_0_), custom_call_target="tpu_custom_call" | custom-call | flops 536870912 | bytes 1048576 | tf_op jit(solution)/shard_map/pallas_call | solution.py:611
  45.0 4.2 %all-to-all-done.3.received = bf16[16,16,128]{2,1,0:T(8,128)(2,1)S(1)} async-done(((bf16[16,16,128]{2,1,0:T(8,128)(2,1)}), bf16[16,16,128]{2,1,0:T(8,128)(2,1)S(1)}, u32[]{:S(2)}, u32[]{:S(2)}) %all-to-all-start.3) | async-done | bytes 65568 | tf_op jit(solution)/shard_map/all_to_all | solution.py:622
  49.2 0.8 %shard_map.144 = f32[6,2048]{1,0:T(8,128)} custom-call(bf16[2,32,256]{2,1,0:T(8,128)(2,1)S(1)} %get-tuple-element.27.pick, f32[6,16,128]{2,1,0:T(8,128)S(1)} %shard_map.143.pushed, bf16[16,16,128]{2,1,0:T(8,128)(2,1)S(1)} %all-to-all-done.3.received, f32[32,128]{1,0:T(8,128)S(1)} %get-tuple-element.37.refs_0_), custom_call_target="tpu_custom_call" | custom-call | flops 65536 | bytes 262144 | tf_op jit(solution)/shard_map/pallas_call | solution.py:656
  (3 shorter events, 0.0 us)
Async XLA Ops:
  0.6 33.7 %copy-start = (f32[512,256]{1,0:T(8,128)S(1)}, f32[512,256]{1,0:T(8,128)}, u32[]{:S(2)}) copy-start(f32[512,256]{1,0:T(8,128)} %z_kernel.1) | copy-start | bytes 1572868
  34.3 7.3 %copy-start.1 = (f32[6,2048]{1,0:T(8,128)S(1)}, f32[6,2048]{1,0:T(8,128)}, u32[]{:S(2)}) copy-start(f32[6,2048]{1,0:T(8,128)} %coords.1) | copy-start | bytes 147460
  34.3 7.4 %copy-start.2 = (f32[6,84]{1,0:T(8,128)S(1)}, f32[6,84]{1,0:T(8,128)}, u32[]{:S(2)}) copy-start(f32[6,84]{1,0:T(8,128)} %transfer.1) | copy-start | bytes 6052
  34.7 1.3 %collective-permute-start = (f32[72,256]{1,0:T(8,128)S(1)}, f32[72,256]{1,0:T(8,128)S(1)}, u32[]{:S(2)}, u32[]{:S(2)}) collective-permute-start(f32[72,256]{1,0:T(8,128)S(1)} %get-tuple-element.32), channel_id=1, source_target_pairs={{0,1},{1,0},{2,3},{3,2},{4,5},{5,4},{6,7},{7,6},{8,9},{9,8},{10,11... | collective-permute-start | bytes 221192 | tf_op jit(solution)/shard_map/ppermute | solution.py:578
  38.2 11.0 %all-to-all-start.3 = ((bf16[16,16,128]{2,1,0:T(8,128)(2,1)}), bf16[16,16,128]{2,1,0:T(8,128)(2,1)S(1)}, u32[]{:S(2)}, u32[]{:S(2)}) async-start(bf16[16,16,128]{2,1,0:T(8,128)(2,1)} %get-tuple-element.33.after), calls=%async_computation.3 | async-start | bytes 131072 | tf_op jit(solution)/shard_map/all_to_all | solution.py:622

commit v2 on v1

--- a/solution.py
+++ b/solution.py
@@ -197,9 +197,18 @@
         (offsets_from, offsets),
         (transfer_from, transfer),
     ]
+    part_rows = min(128, slab_rows)
+    tops = range(0, slab_rows, part_rows)
+    arrival = {}
     for comp in range(comps):
-        pairs += [(history.at[t, comp], frames.at[t, comp]) for t in range(count_steps)]
+        for top in tops:
+            part = pl.ds(top, part_rows)
+            arrival[comp, top] = len(pairs)
+            pairs += [
+                (history.at[t, comp, part], frames.at[t, comp, part]) for t in range(count_steps)
+            ]
         if comp == 0:
+            x_arrival = len(pairs)
             pairs += [(x_kernel, x_here)]
     fetch = [
         pltpu.make_async_copy(source, target, sems.at[index])
@@ -252,12 +261,10 @@
                     later[partner, :, lanes] = value.astype(later.dtype)
 
     for comp in range(comps):
-        first = 9 + comp * (count_steps + 1)
-        for copy in fetch[first : first + count_steps]:
-            copy.wait()
         here = slice(comp * slab_rows, (comp + 1) * slab_rows)
-        part_rows = min(128, slab_rows)
-        for top in range(0, slab_rows, part_rows):
+        for top in tops:
+            for t in range(count_steps):
+                fetch[arrival[comp, top] + t].wait()
             for q in range(width // LANES):
                 before = slice(LANES * max(q - 1, 0), LANES * (q + 1))
                 steps = [
@@ -278,7 +285,7 @@
             if rounds == 2:
                 store(later, later_to)
             store(packed.at[:, spread_rows:], packed_to.at[:, spread_rows:])
-            fetch[9 + count_steps].wait()
+            fetch[x_arrival].wait()
             high, low = split(x_here[...])
             x_parts[:width] = high
             x_parts[width : 2 * width] = high
@@ -544,7 +551,7 @@
             pltpu.SMEM((1, strips), jnp.int32),
             pltpu.VMEM((rounds, comps * blocks, comps * strips * seats), bf16),
             pltpu.VMEM((FIELDS * (rounds * strips * seats + 2), LANES), f32),
-            pltpu.SemaphoreType.DMA((16 + comps * count_steps,)),
+            pltpu.SemaphoreType.DMA((16 + 2 * comps * count_steps,)),
         ],
         flops=6 * comps * slab_rows * width * width,
         moved=history.size * 2 + x_kernel.size * 4,

time: 50.3 us -> 51.1 us (1.016)
    pallas_call x1, Pallas kernels: 6.63 us -> 7.63 us  [local(): call(functools.partial(source_kernel, strips), (jax.ShapeDtypeStruct((str...]
  transfers between devices with their start and end apart: 2 -> 2, of which waited for: 2 -> 2; matrix products, arithmetic and copies ran while one was open for 0% -> 0% of each run, Pallas kernels for 9% -> 8%
where the time goes in v2:
time: 51.1 us; the launch traced here: 50.6 us
  blocking collectives  27.1 us (53%)
  Pallas kernels  14.4 us (28%)
  waiting for transfers between devices  4.84 us (9%)
  starting transfers between devices  3.58 us (7%)
  between operations  0.75 us (1%)
    all_to_all x1, blocking collectives, local(): arrived = lax.all_to_all(packed, 'hist', 0, 0, tiled=True)  27.1 us
    pallas_call x1, Pallas kernels, local(): call(functools.partial(source_kernel, strips), (jax.ShapeDtypeStruct((str...  7.63 us
    all_to_all x1, waiting for transfers between devices, exchange(): return lax.all_to_all(value, 'hist', 0, 0, tiled=True)  4.68 us
    all_to_all x1, starting transfers between devices, exchange(): return lax.all_to_all(value, 'hist', 0, 0, tiled=True)  3.51 us
    pallas_call x1, Pallas kernels, deposits(): call(functools.partial(deposit_kernel, seats), jax.ShapeDtypeStruct((comp...  1.72 us
    pallas_call x1, Pallas kernels, sample(): call(functools.partial(sample_kernel, seats), (jax.ShapeDtypeStruct((comp...  1.68 us
    pallas_call x1, Pallas kernels, unpack(): call(functools.partial(unpack_kernel, spread_rows), (jax.ShapeDtypeStruct...  1.09 us
    pallas_call x1, Pallas kernels, local(): call(push_kernel, jax.ShapeDtypeStruct((6,) + tile, f32), [SMEM, VMEM, HB...  1.08 us
  transfers between devices with their start and end apart: 2, of which 2 were waited for; matrix products, arithmetic and copies ran while one was open for 0% of the time, Pallas kernels for 8%

profile of v2, /device:TPU:0, one launch (start us, length us, event | category | flops | bytes accessed | tf_op | source)
XLA Modules:
  0.0 50.6 jit_solution(11460154426036413366)
XLA Ops:
  0.6 0.0 copy-start
  0.6 7.6 %shard_map.139 = (bf16[16,80,256]{2,1,0:T(8,128)(2,1)}, bf16[16,16,256]{2,1,0:T(8,128)(2,1)S(1)}, bf16[2,32,256]{2,1,0:T(8,128)(2,1)S(1)}) custom-call(s32[1,16]{1,0:T(1,128)} %bitcast.16, s32[1,8]{1,0:T(1,128)} %bitcast.17, f32[1,8]{1,0:T(1,128)} %bitcast.18, f32[1,8]{1,0:T(1,128)} %bitcast.19, f32[6,2048]{1,0:T(8,128)} %coords.1, f32[16,128]{1,0:T(8,128)} %bitcast.13, ...), custom_call_target="tpu_custom_call" | custom-call | flops 805306368 | bytes 5242880 | tf_op jit(solution)/shard_map/pallas_call | solution.py:523
  8.3 27.1 %all_to_all.19.arrived = bf16[16,80,256]{2,1,0:T(8,128)(2,1)S(1)} all-to-all(bf16[16,80,256]{2,1,0:T(8,128)(2,1)} %get-tuple-element.28), channel_id=1, replica_groups=mesh['hist'=16,'dom'=2] {'hist'}, dimensions={0} | all-to-all | bytes 1310720 | tf_op jit(solution)/shard_map/all_to_all | solution.py:572
  35.3 0.0 copy-done
  35.3 0.0 copy-start.1
  35.3 0.0 copy-start.2
  35.3 0.4 shard_map.141
  35.7 0.1 collective-permute-start
  35.8 1.1 %shard_map.140 = (f32[17,32,128]{2,1,0:T(8,128)S(1)}, s32[160]{0:T(256)S(1)}) custom-call(bf16[16,80,256]{2,1,0:T(8,128)(2,1)S(1)} %all_to_all.19.arrived), custom_call_target="tpu_custom_call" | custom-call | flops 1048576 | bytes 1048576 | tf_op jit(solution)/shard_map/pallas_call | solution.py:590
  36.9 0.2 collective-permute-done.refs_1_
  37.1 1.7 %shard_map.142 = (f32[2,32,256]{2,1,0:T(8,128)}, bf16[16,16,128]{2,1,0:T(8,128)(2,1)}, s32[8]{0:T(128)S(1)}) custom-call(s32[160]{0:T(256)S(1)} %get-tuple-element.29.chosen, f32[17,32,128]{2,1,0:T(8,128)S(1)} %get-tuple-element.30.records, f32[72,256]{1,0:T(8,128)S(1)} %get-tuple-element.31.refs_0_, f32[72,256]{1,0:T(8,128)S(1)} %collective-permute-done.refs_1_), custom_call_target="tpu_custom_call" | custom-call | flops 536870912 | bytes 1048576 | tf_op jit(solution)/shard_map/pallas_call | solution.py:603
  38.8 3.5 %all-to-all-start.3 = ((bf16[16,16,128]{2,1,0:T(8,128)(2,1)}), bf16[16,16,128]{2,1,0:T(8,128)(2,1)S(1)}, u32[]{:S(2)}, u32[]{:S(2)}) async-start(bf16[16,16,128]{2,1,0:T(8,128)(2,1)} %get-tuple-element.33.after), calls=%async_computation.3 | async-start | bytes 131072 | tf_op jit(solution)/shard_map/all_to_all | solution.py:629
  42.3 0.0 copy-done.1
  42.4 0.0 copy-done.2
  42.4 1.1 %shard_map.143.pushed = f32[6,16,128]{2,1,0:T(8,128)S(1)} custom-call(f32[6,84]{1,0:T(8,128)S(1)} %copy-done.2, f32[6,2048]{1,0:T(8,128)S(1)} %copy-done.1, bf16[16,16,128]{2,1,0:T(8,128)(2,1)} %get-tuple-element.33.after), custom_call_target="tpu_custom_call" | custom-call | flops 2457600 | bytes 262144 | tf_op jit(solution)/shard_map/pallas_call | solution.py:655
  43.4 1.7 %shard_map.145 = f32[2,32,256]{2,1,0:T(8,128)} custom-call(s32[160]{0:T(256)S(1)} %get-tuple-element.29.chosen, f32[17,32,128]{2,1,0:T(8,128)S(1)} %get-tuple-element.30.records, bf16[16,16,128]{2,1,0:T(8,128)(2,1)} %get-tuple-element.33.after, f32[2,32,256]{2,1,0:T(8,128)S(1)} %get-tuple-element.38.refs_0_), custom_call_target="tpu_custom_call" | custom-call | flops 536870912 | bytes 1048576 | tf_op jit(solution)/shard_map/pallas_call | solution.py:618
  45.2 4.7 %all-to-all-done.3.received = bf16[16,16,128]{2,1,0:T(8,128)(2,1)S(1)} async-done(((bf16[16,16,128]{2,1,0:T(8,128)(2,1)}), bf16[16,16,128]{2,1,0:T(8,128)(2,1)S(1)}, u32[]{:S(2)}, u32[]{:S(2)}) %all-to-all-start.3) | async-done | bytes 65568 | tf_op jit(solution)/shard_map/all_to_all | solution.py:629
  49.8 0.8 %shard_map.144 = f32[6,2048]{1,0:T(8,128)} custom-call(bf16[2,32,256]{2,1,0:T(8,128)(2,1)S(1)} %get-tuple-element.27.pick, f32[6,16,128]{2,1,0:T(8,128)S(1)} %shard_map.143.pushed, bf16[16,16,128]{2,1,0:T(8,128)(2,1)S(1)} %all-to-all-done.3.received, f32[32,128]{1,0:T(8,128)S(1)} %get-tuple-element.37.refs_0_), custom_call_target="tpu_custom_call" | custom-call | flops 65536 | bytes 262144 | tf_op jit(solution)/shard_map/pallas_call | solution.py:663
  (3 shorter events, 0.0 us)
Async XLA Ops:
  0.6 34.7 %copy-start = (f32[512,256]{1,0:T(8,128)S(1)}, f32[512,256]{1,0:T(8,128)}, u32[]{:S(2)}) copy-start(f32[512,256]{1,0:T(8,128)} %z_kernel.1) | copy-start | bytes 1572868
  35.3 7.0 %copy-start.1 = (f32[6,2048]{1,0:T(8,128)S(1)}, f32[6,2048]{1,0:T(8,128)}, u32[]{:S(2)}) copy-start(f32[6,2048]{1,0:T(8,128)} %coords.1) | copy-start | bytes 147460
  35.3 7.0 %copy-start.2 = (f32[6,84]{1,0:T(8,128)S(1)}, f32[6,84]{1,0:T(8,128)}, u32[]{:S(2)}) copy-start(f32[6,84]{1,0:T(8,128)} %transfer.1) | copy-start | bytes 6052
  35.7 1.3 %collective-permute-start = (f32[72,256]{1,0:T(8,128)S(1)}, f32[72,256]{1,0:T(8,128)S(1)}, u32[]{:S(2)}, u32[]{:S(2)}) collective-permute-start(f32[72,256]{1,0:T(8,128)S(1)} %get-tuple-element.32), channel_id=1, source_target_pairs={{0,1},{1,0},{2,3},{3,2},{4,5},{5,4},{6,7},{7,6},{8,9},{9,8},{10,11... | collective-permute-start | bytes 221192 | tf_op jit(solution)/shard_map/ppermute | solution.py:585
  38.8 11.0 %all-to-all-start.3 = ((bf16[16,16,128]{2,1,0:T(8,128)(2,1)}), bf16[16,16,128]{2,1,0:T(8,128)(2,1)S(1)}, u32[]{:S(2)}, u32[]{:S(2)}) async-start(bf16[16,16,128]{2,1,0:T(8,128)(2,1)} %get-tuple-element.33.after), calls=%async_computation.3 | async-start | bytes 131072 | tf_op jit(solution)/shard_map/all_to_all | solution.py:629

commit v3 on v1

--- a/solution.py
+++ b/solution.py
@@ -198,7 +198,7 @@
         (transfer_from, transfer),
     ]
     for comp in range(comps):
-        pairs += [(history.at[t, comp], frames.at[t, comp]) for t in range(count_steps)]
+        pairs += [(history.at[:, comp], frames.at[:, comp])]
         if comp == 0:
             pairs += [(x_kernel, x_here)]
     fetch = [
@@ -252,9 +252,7 @@
                     later[partner, :, lanes] = value.astype(later.dtype)
 
     for comp in range(comps):
-        first = 9 + comp * (count_steps + 1)
-        for copy in fetch[first : first + count_steps]:
-            copy.wait()
+        fetch[9 + (comp + 1 if comp else 0)].wait()
         here = slice(comp * slab_rows, (comp + 1) * slab_rows)
         part_rows = min(128, slab_rows)
         for top in range(0, slab_rows, part_rows):
@@ -278,7 +276,7 @@
             if rounds == 2:
                 store(later, later_to)
             store(packed.at[:, spread_rows:], packed_to.at[:, spread_rows:])
-            fetch[9 + count_steps].wait()
+            fetch[10].wait()
             high, low = split(x_here[...])
             x_parts[:width] = high
             x_parts[width : 2 * width] = high
@@ -544,7 +542,7 @@
             pltpu.SMEM((1, strips), jnp.int32),
             pltpu.VMEM((rounds, comps * blocks, comps * strips * seats), bf16),
             pltpu.VMEM((FIELDS * (rounds * strips * seats + 2), LANES), f32),
-            pltpu.SemaphoreType.DMA((16 + comps * count_steps,)),
+            pltpu.SemaphoreType.DMA((20,)),
         ],
         flops=6 * comps * slab_rows * width * width,
         moved=history.size * 2 + x_kernel.size * 4,

time: 50.3 us -> 50.2 us (level)
  no operation moved by 1% of the time
where the time goes in v3:
time: 50.2 us; the launch traced here: 49.9 us
  blocking collectives  27.1 us (54%)
  Pallas kernels  14.1 us (28%)
  waiting for transfers between devices  4.39 us (9%)
  starting transfers between devices  3.58 us (7%)
  between operations  0.75 us (1%)
    all_to_all x1, blocking collectives, local(): arrived = lax.all_to_all(packed, 'hist', 0, 0, tiled=True)  27.1 us
    pallas_call x1, Pallas kernels, local(): call(functools.partial(source_kernel, strips), (jax.ShapeDtypeStruct((str...  6.52 us
    all_to_all x1, waiting for transfers between devices, exchange(): return lax.all_to_all(value, 'hist', 0, 0, tiled=True)  4.24 us
    all_to_all x1, starting transfers between devices, exchange(): return lax.all_to_all(value, 'hist', 0, 0, tiled=True)  3.51 us
    pallas_call x1, Pallas kernels, deposits(): call(functools.partial(deposit_kernel, seats), jax.ShapeDtypeStruct((comp...  2.17 us
    pallas_call x1, Pallas kernels, sample(): call(functools.partial(sample_kernel, seats), (jax.ShapeDtypeStruct((comp...  2.03 us
    pallas_call x1, Pallas kernels, unpack(): call(functools.partial(unpack_kernel, spread_rows), (jax.ShapeDtypeStruct...  1.09 us
    pallas_call x1, Pallas kernels, local(): call(push_kernel, jax.ShapeDtypeStruct((6,) + tile, f32), [SMEM, VMEM, HB...  1.08 us
  transfers between devices with their start and end apart: 2, of which 2 were waited for; matrix products, arithmetic and copies ran while one was open for 0% of the time, Pallas kernels for 9%

profile of v3, /device:TPU:0, one launch (start us, length us, event | category | flops | bytes accessed | tf_op | source)
XLA Modules:
  0.0 49.9 jit_solution(3971095399649814677)
XLA Ops:
  0.6 0.0 copy-start
  0.6 6.5 %shard_map.139 = (bf16[16,80,256]{2,1,0:T(8,128)(2,1)}, bf16[16,16,256]{2,1,0:T(8,128)(2,1)S(1)}, bf16[2,32,256]{2,1,0:T(8,128)(2,1)S(1)}) custom-call(s32[1,16]{1,0:T(1,128)} %bitcast.16, s32[1,8]{1,0:T(1,128)} %bitcast.17, f32[1,8]{1,0:T(1,128)} %bitcast.18, f32[1,8]{1,0:T(1,128)} %bitcast.19, f32[6,2048]{1,0:T(8,128)} %coords.1, f32[16,128]{1,0:T(8,128)} %bitcast.13, ...), custom_call_target="tpu_custom_call" | custom-call | flops 805306368 | bytes 5242880 | tf_op jit(solution)/shard_map/pallas_call | solution.py:514
  7.2 27.1 %all_to_all.19.arrived = bf16[16,80,256]{2,1,0:T(8,128)(2,1)S(1)} all-to-all(bf16[16,80,256]{2,1,0:T(8,128)(2,1)} %get-tuple-element.28), channel_id=1, replica_groups=mesh['hist'=16,'dom'=2] {'hist'}, dimensions={0} | all-to-all | bytes 1310720 | tf_op jit(solution)/shard_map/all_to_all | solution.py:563
  34.2 0.0 copy-done
  34.2 0.0 copy-start.1
  34.2 0.0 copy-start.2
  34.2 0.4 shard_map.141
  34.6 0.1 collective-permute-start
  34.7 1.1 %shard_map.140 = (f32[17,32,128]{2,1,0:T(8,128)S(1)}, s32[160]{0:T(256)S(1)}) custom-call(bf16[16,80,256]{2,1,0:T(8,128)(2,1)S(1)} %all_to_all.19.arrived), custom_call_target="tpu_custom_call" | custom-call | flops 1048576 | bytes 1048576 | tf_op jit(solution)/shard_map/pallas_call | solution.py:581
  35.8 0.2 collective-permute-done.refs_1_
  35.9 2.0 %shard_map.142 = (f32[2,32,256]{2,1,0:T(8,128)}, bf16[16,16,128]{2,1,0:T(8,128)(2,1)}, s32[8]{0:T(128)S(1)}) custom-call(s32[160]{0:T(256)S(1)} %get-tuple-element.29.chosen, f32[17,32,128]{2,1,0:T(8,128)S(1)} %get-tuple-element.30.records, f32[72,256]{1,0:T(8,128)S(1)} %get-tuple-element.31.refs_0_, f32[72,256]{1,0:T(8,128)S(1)} %collective-permute-done.refs_1_), custom_call_target="tpu_custom_call" | custom-call | flops 536870912 | bytes 1048576 | tf_op jit(solution)/shard_map/pallas_call | solution.py:594
  38.1 3.5 %all-to-all-start.3 = ((bf16[16,16,128]{2,1,0:T(8,128)(2,1)}), bf16[16,16,128]{2,1,0:T(8,128)(2,1)S(1)}, u32[]{:S(2)}, u32[]{:S(2)}) async-start(bf16[16,16,128]{2,1,0:T(8,128)(2,1)} %get-tuple-element.33.after), calls=%async_computation.3 | async-start | bytes 131072 | tf_op jit(solution)/shard_map/all_to_all | solution.py:620
  41.6 0.0 copy-done.1
  41.6 0.0 copy-done.2
  41.6 1.1 %shard_map.143.pushed = f32[6,16,128]{2,1,0:T(8,128)S(1)} custom-call(f32[6,84]{1,0:T(8,128)S(1)} %copy-done.2, f32[6,2048]{1,0:T(8,128)S(1)} %copy-done.1, bf16[16,16,128]{2,1,0:T(8,128)(2,1)} %get-tuple-element.33.after), custom_call_target="tpu_custom_call" | custom-call | flops 2457600 | bytes 262144 | tf_op jit(solution)/shard_map/pallas_call | solution.py:646
  42.7 2.2 %shard_map.145 = f32[2,32,256]{2,1,0:T(8,128)} custom-call(s32[160]{0:T(256)S(1)} %get-tuple-element.29.chosen, f32[17,32,128]{2,1,0:T(8,128)S(1)} %get-tuple-element.30.records, bf16[16,16,128]{2,1,0:T(8,128)(2,1)} %get-tuple-element.33.after, f32[2,32,256]{2,1,0:T(8,128)S(1)} %get-tuple-element.38.refs_0_), custom_call_target="tpu_custom_call" | custom-call | flops 536870912 | bytes 1048576 | tf_op jit(solution)/shard_map/pallas_call | solution.py:609
  44.8 4.2 %all-to-all-done.3.received = bf16[16,16,128]{2,1,0:T(8,128)(2,1)S(1)} async-done(((bf16[16,16,128]{2,1,0:T(8,128)(2,1)}), bf16[16,16,128]{2,1,0:T(8,128)(2,1)S(1)}, u32[]{:S(2)}, u32[]{:S(2)}) %all-to-all-start.3) | async-done | bytes 65568 | tf_op jit(solution)/shard_map/all_to_all | solution.py:620
  49.1 0.8 %shard_map.144 = f32[6,2048]{1,0:T(8,128)} custom-call(bf16[2,32,256]{2,1,0:T(8,128)(2,1)S(1)} %get-tuple-element.27.pick, f32[6,16,128]{2,1,0:T(8,128)S(1)} %shard_map.143.pushed, bf16[16,16,128]{2,1,0:T(8,128)(2,1)S(1)} %all-to-all-done.3.received, f32[32,128]{1,0:T(8,128)S(1)} %get-tuple-element.37.refs_0_), custom_call_target="tpu_custom_call" | custom-call | flops 65536 | bytes 262144 | tf_op jit(solution)/shard_map/pallas_call | solution.py:654
  (3 shorter events, 0.0 us)
Async XLA Ops:
  0.6 33.6 %copy-start = (f32[512,256]{1,0:T(8,128)S(1)}, f32[512,256]{1,0:T(8,128)}, u32[]{:S(2)}) copy-start(f32[512,256]{1,0:T(8,128)} %z_kernel.1) | copy-start | bytes 1572868
  34.2 7.3 %copy-start.1 = (f32[6,2048]{1,0:T(8,128)S(1)}, f32[6,2048]{1,0:T(8,128)}, u32[]{:S(2)}) copy-start(f32[6,2048]{1,0:T(8,128)} %coords.1) | copy-start | bytes 147460
  34.2 7.4 %copy-start.2 = (f32[6,84]{1,0:T(8,128)S(1)}, f32[6,84]{1,0:T(8,128)}, u32[]{:S(2)}) copy-start(f32[6,84]{1,0:T(8,128)} %transfer.1) | copy-start | bytes 6052
  34.6 1.3 %collective-permute-start = (f32[72,256]{1,0:T(8,128)S(1)}, f32[72,256]{1,0:T(8,128)S(1)}, u32[]{:S(2)}, u32[]{:S(2)}) collective-permute-start(f32[72,256]{1,0:T(8,128)S(1)} %get-tuple-element.32), channel_id=1, source_target_pairs={{0,1},{1,0},{2,3},{3,2},{4,5},{5,4},{6,7},{7,6},{8,9},{9,8},{10,11... | collective-permute-start | bytes 221192 | tf_op jit(solution)/shard_map/ppermute | solution.py:576
  38.1 11.0 %all-to-all-start.3 = ((bf16[16,16,128]{2,1,0:T(8,128)(2,1)}), bf16[16,16,128]{2,1,0:T(8,128)(2,1)S(1)}, u32[]{:S(2)}, u32[]{:S(2)}) async-start(bf16[16,16,128]{2,1,0:T(8,128)(2,1)} %get-tuple-element.33.after), calls=%async_computation.3 | async-start | bytes 131072 | tf_op jit(solution)/shard_map/all_to_all | solution.py:620

commit v4 on v3

--- a/solution.py
+++ b/solution.py
@@ -205,7 +205,8 @@
         pltpu.make_async_copy(source, target, sems.at[index])
         for index, (source, target) in enumerate(pairs)
     ]
-    for copy in fetch:
+    fetch[9].start()
+    for copy in fetch[:9] + fetch[10:]:
         copy.start()
     stored = []
 

time: 50.2 us -> 50.7 us (level)
  waiting for transfers between devices: 4.39 us -> 5.09 us
    all_to_all x1, waiting for transfers between devices: 4.24 us -> 4.94 us  [exchange(): return lax.all_to_all(value, 'hist', 0, 0, tiled=True)]
    pallas_call x1, Pallas kernels: 6.52 us -> 7.13 us  [local(): call(functools.partial(source_kernel, strips), (jax.ShapeDtypeStruct((str...]
  transfers between devices with their start and end apart: 2 -> 2, of which waited for: 2 -> 2; matrix products, arithmetic and copies ran while one was open for 0% -> 0% of each run, Pallas kernels for 9% -> 8%
where the time goes in v4:
time: 50.7 us; the launch traced here: 50.4 us
  blocking collectives  27.1 us (53%)
  Pallas kernels  13.9 us (27%)
  waiting for transfers between devices  5.09 us (10%)
  starting transfers between devices  3.58 us (7%)
  between operations  0.75 us (1%)
    all_to_all x1, blocking collectives, local(): arrived = lax.all_to_all(packed, 'hist', 0, 0, tiled=True)  27.1 us
    pallas_call x1, Pallas kernels, local(): call(functools.partial(source_kernel, strips), (jax.ShapeDtypeStruct((str...  7.13 us
    all_to_all x1, waiting for transfers between devices, exchange(): return lax.all_to_all(value, 'hist', 0, 0, tiled=True)  4.94 us
    all_to_all x1, starting transfers between devices, exchange(): return lax.all_to_all(value, 'hist', 0, 0, tiled=True)  3.51 us
    pallas_call x1, Pallas kernels, deposits(): call(functools.partial(deposit_kernel, seats), jax.ShapeDtypeStruct((comp...  1.72 us
    pallas_call x1, Pallas kernels, sample(): call(functools.partial(sample_kernel, seats), (jax.ShapeDtypeStruct((comp...  1.68 us
    pallas_call x1, Pallas kernels, unpack(): call(functools.partial(unpack_kernel, spread_rows), (jax.ShapeDtypeStruct...  1.09 us
    pallas_call x1, Pallas kernels, local(): call(push_kernel, jax.ShapeDtypeStruct((6,) + tile, f32), [SMEM, VMEM, HB...  1.08 us
  transfers between devices with their start and end apart: 2, of which 2 were waited for; matrix products, arithmetic and copies ran while one was open for 0% of the time, Pallas kernels for 8%

profile of v4, /device:TPU:0, one launch (start us, length us, event | category | flops | bytes accessed | tf_op | source)
XLA Modules:
  0.0 50.4 jit_solution(16881617551403585939)
XLA Ops:
  0.6 0.0 copy-start
  0.6 7.1 %shard_map.139 = (bf16[16,80,256]{2,1,0:T(8,128)(2,1)}, bf16[16,16,256]{2,1,0:T(8,128)(2,1)S(1)}, bf16[2,32,256]{2,1,0:T(8,128)(2,1)S(1)}) custom-call(s32[1,16]{1,0:T(1,128)} %bitcast.16, s32[1,8]{1,0:T(1,128)} %bitcast.17, f32[1,8]{1,0:T(1,128)} %bitcast.18, f32[1,8]{1,0:T(1,128)} %bitcast.19, f32[6,2048]{1,0:T(8,128)} %coords.1, f32[16,128]{1,0:T(8,128)} %bitcast.13, ...), custom_call_target="tpu_custom_call" | custom-call | flops 805306368 | bytes 5242880 | tf_op jit(solution)/shard_map/pallas_call | solution.py:515
  7.8 27.1 %all_to_all.19.arrived = bf16[16,80,256]{2,1,0:T(8,128)(2,1)S(1)} all-to-all(bf16[16,80,256]{2,1,0:T(8,128)(2,1)} %get-tuple-element.28), channel_id=1, replica_groups=mesh['hist'=16,'dom'=2] {'hist'}, dimensions={0} | all-to-all | bytes 1310720 | tf_op jit(solution)/shard_map/all_to_all | solution.py:564
  34.8 0.0 copy-done
  34.8 0.0 copy-start.1
  34.8 0.0 copy-start.2
  34.8 0.4 shard_map.141
  35.2 0.1 collective-permute-start
  35.3 1.1 %shard_map.140 = (f32[17,32,128]{2,1,0:T(8,128)S(1)}, s32[160]{0:T(256)S(1)}) custom-call(bf16[16,80,256]{2,1,0:T(8,128)(2,1)S(1)} %all_to_all.19.arrived), custom_call_target="tpu_custom_call" | custom-call | flops 1048576 | bytes 1048576 | tf_op jit(solution)/shard_map/pallas_call | solution.py:582
  36.4 0.2 collective-permute-done.refs_1_
  36.5 1.7 %shard_map.142 = (f32[2,32,256]{2,1,0:T(8,128)}, bf16[16,16,128]{2,1,0:T(8,128)(2,1)}, s32[8]{0:T(128)S(1)}) custom-call(s32[160]{0:T(256)S(1)} %get-tuple-element.29.chosen, f32[17,32,128]{2,1,0:T(8,128)S(1)} %get-tuple-element.30.records, f32[72,256]{1,0:T(8,128)S(1)} %get-tuple-element.31.refs_0_, f32[72,256]{1,0:T(8,128)S(1)} %collective-permute-done.refs_1_), custom_call_target="tpu_custom_call" | custom-call | flops 536870912 | bytes 1048576 | tf_op jit(solution)/shard_map/pallas_call | solution.py:595
  38.3 3.5 %all-to-all-start.3 = ((bf16[16,16,128]{2,1,0:T(8,128)(2,1)}), bf16[16,16,128]{2,1,0:T(8,128)(2,1)S(1)}, u32[]{:S(2)}, u32[]{:S(2)}) async-start(bf16[16,16,128]{2,1,0:T(8,128)(2,1)} %get-tuple-element.33.after), calls=%async_computation.3 | async-start | bytes 131072 | tf_op jit(solution)/shard_map/all_to_all | solution.py:621
  41.8 0.0 copy-done.1
  41.9 0.0 copy-done.2
  41.9 1.1 %shard_map.143.pushed = f32[6,16,128]{2,1,0:T(8,128)S(1)} custom-call(f32[6,84]{1,0:T(8,128)S(1)} %copy-done.2, f32[6,2048]{1,0:T(8,128)S(1)} %copy-done.1, bf16[16,16,128]{2,1,0:T(8,128)(2,1)} %get-tuple-element.33.after), custom_call_target="tpu_custom_call" | custom-call | flops 2457600 | bytes 262144 | tf_op jit(solution)/shard_map/pallas_call | solution.py:647
  42.9 1.7 %shard_map.145 = f32[2,32,256]{2,1,0:T(8,128)} custom-call(s32[160]{0:T(256)S(1)} %get-tuple-element.29.chosen, f32[17,32,128]{2,1,0:T(8,128)S(1)} %get-tuple-element.30.records, bf16[16,16,128]{2,1,0:T(8,128)(2,1)} %get-tuple-element.33.after, f32[2,32,256]{2,1,0:T(8,128)S(1)} %get-tuple-element.38.refs_0_), custom_call_target="tpu_custom_call" | custom-call | flops 536870912 | bytes 1048576 | tf_op jit(solution)/shard_map/pallas_call | solution.py:610
  44.7 4.9 %all-to-all-done.3.received = bf16[16,16,128]{2,1,0:T(8,128)(2,1)S(1)} async-done(((bf16[16,16,128]{2,1,0:T(8,128)(2,1)}), bf16[16,16,128]{2,1,0:T(8,128)(2,1)S(1)}, u32[]{:S(2)}, u32[]{:S(2)}) %all-to-all-start.3) | async-done | bytes 65568 | tf_op jit(solution)/shard_map/all_to_all | solution.py:621
  49.6 0.8 %shard_map.144 = f32[6,2048]{1,0:T(8,128)} custom-call(bf16[2,32,256]{2,1,0:T(8,128)(2,1)S(1)} %get-tuple-element.27.pick, f32[6,16,128]{2,1,0:T(8,128)S(1)} %shard_map.143.pushed, bf16[16,16,128]{2,1,0:T(8,128)(2,1)S(1)} %all-to-all-done.3.received, f32[32,128]{1,0:T(8,128)S(1)} %get-tuple-element.37.refs_0_), custom_call_target="tpu_custom_call" | custom-call | flops 65536 | bytes 262144 | tf_op jit(solution)/shard_map/pallas_call | solution.py:655
  (3 shorter events, 0.0 us)
Async XLA Ops:
  0.6 34.2 %copy-start = (f32[512,256]{1,0:T(8,128)S(1)}, f32[512,256]{1,0:T(8,128)}, u32[]{:S(2)}) copy-start(f32[512,256]{1,0:T(8,128)} %z_kernel.1) | copy-start | bytes 1572868
  34.8 7.0 %copy-start.1 = (f32[6,2048]{1,0:T(8,128)S(1)}, f32[6,2048]{1,0:T(8,128)}, u32[]{:S(2)}) copy-start(f32[6,2048]{1,0:T(8,128)} %coords.1) | copy-start | bytes 147460
  34.8 7.0 %copy-start.2 = (f32[6,84]{1,0:T(8,128)S(1)}, f32[6,84]{1,0:T(8,128)}, u32[]{:S(2)}) copy-start(f32[6,84]{1,0:T(8,128)} %transfer.1) | copy-start | bytes 6052
  35.2 1.3 %collective-permute-start = (f32[72,256]{1,0:T(8,128)S(1)}, f32[72,256]{1,0:T(8,128)S(1)}, u32[]{:S(2)}, u32[]{:S(2)}) collective-permute-start(f32[72,256]{1,0:T(8,128)S(1)} %get-tuple-element.32), channel_id=1, source_target_pairs={{0,1},{1,0},{2,3},{3,2},{4,5},{5,4},{6,7},{7,6},{8,9},{9,8},{10,11... | collective-permute-start | bytes 221192 | tf_op jit(solution)/shard_map/ppermute | solution.py:577
  38.3 11.3 %all-to-all-start.3 = ((bf16[16,16,128]{2,1,0:T(8,128)(2,1)}), bf16[16,16,128]{2,1,0:T(8,128)(2,1)S(1)}, u32[]{:S(2)}, u32[]{:S(2)}) async-start(bf16[16,16,128]{2,1,0:T(8,128)(2,1)} %get-tuple-element.33.after), calls=%async_computation.3 | async-start | bytes 131072 | tf_op jit(solution)/shard_map/all_to_all | solution.py:621
